TPU v7x, 256 devices: a whole 4x4x8 slice. The times are simulated.
256 devices in a mesh: row: 32 (over z_lo, x, y), col: 8 (over z_hi, core).
Axes of the slice: x: 4, y: 4, z: 8 (z_hi: 4, z_lo: 2; z = z_hi * 2 + z_lo), core: 2. Of those that a mesh axis runs over, the one named last changes fastest.
Arguments:
- grad_out: bfloat16 [64, 512, 2048], P(None, 'row', 'col'), may hold values from -6 to 6
- row_feat: bfloat16 [512, 64], P('row'), may hold values from -6 to 6
- col_feat: bfloat16 [2048, 64], P('col'), may hold values from -6 to 6
- conv_one: bfloat16 [3, 3, 64, 64], replicated, may hold values from -0.25 to 0.25
- bias_one: float32 [64], replicated, may hold values from -3 to 3
- conv_two: bfloat16 [3, 3, 64, 64], replicated, may hold values from -0.25 to 0.25
Outputs:
- row_grad: float32 [512, 64], P('row')
- col_grad: float32 [2048, 64], P('col')
- grad_conv_one: float32 [3, 3, 64, 64], replicated
- grad_bias: float32 [64], replicated
- grad_conv_two: float32 [3, 3, 64, 64], replicated
All inputs are finite; a program needn't handle non-finite values.
Results may differ from a plain program's by a relative error of at most 0.0065.
Values may be sent and summed in bfloat16 or wider, within the bound.
No kernel may reach another device: no remote copies, remote signals or barrier semaphores. Data moves between devices by JAX's collectives and lax.ppermute only.
A program may use at most 128 MiB of HBM per device.

v0:
```python
import math
import jax
import jax.numpy as jnp
from jax import lax
from jax.sharding import PartitionSpec as P


def extended(block, sides, width):
    for axis, dim in sides:
        count = lax.axis_size(axis)
        forward = [(i, i + 1) for i in range(count - 1)]
        backward = [(target, source) for source, target in forward]
        low = lax.ppermute(
            lax.slice_in_dim(block, block.shape[dim] - width, None, axis=dim), axis, forward
        )
        high = lax.ppermute(lax.slice_in_dim(block, 0, width, axis=dim), axis, backward)
        block = jnp.concatenate([low, block, high], axis=dim)
    return block


def conv_valid(kernel, field):
    result = lax.conv_general_dilated(
        field[None],
        kernel,
        (1, 1),
        "VALID",
        rhs_dilation=(8, 8),
        dimension_numbers=("NCHW", "HWOI", "NCHW"),
        preferred_element_type=jnp.float32,
    )
    return result[0]


def flipped(kernel):
    return jnp.transpose(kernel[::-1, ::-1], (0, 1, 3, 2))


def tap_grads(upper, field, base_r, base_c, rows, cols):
    taps = []
    for tap_r in range(3):
        line = []
        for tap_c in range(3):
            top = base_r + 8 * (tap_r - 1)
            left = base_c + 8 * (tap_c - 1)
            piece = field[:, top : top + rows, left : left + cols]
            line.append(
                lax.dot_general(
                    upper, piece, (((1, 2), (1, 2)), ((), ())), preferred_element_type=jnp.float32
                )
            )
        taps.append(jnp.stack(line))
    return jnp.stack(taps)


def slope(pre):
    sig = jax.nn.sigmoid(pre)
    return sig * (1.0 + pre * (1.0 - sig))


def inside_mask(row_first, col_first, margin, tile_rows, tile_cols, total_rows, total_cols):
    global_rows = row_first + jnp.arange(tile_rows + 2 * margin, dtype=jnp.int32) - margin
    global_cols = col_first + jnp.arange(tile_cols + 2 * margin, dtype=jnp.int32) - margin
    return ((global_rows >= 0) & (global_rows < total_rows))[:, None] & (
        (global_cols >= 0) & (global_cols < total_cols)
    )[None, :]


def shards(grad_out, row_feat, col_feat, conv_one, bias_one, conv_two):
    chans, tile_rows, tile_cols = grad_out.shape
    total_rows = tile_rows * lax.axis_size("row")
    total_cols = tile_cols * lax.axis_size("col")
    row_first = lax.axis_index("row") * tile_rows
    col_first = lax.axis_index("col") * tile_cols
    row_ext = extended(row_feat, (("row", 0),), 16)
    col_ext = extended(col_feat, (("col", 0),), 16)
    outer = inside_mask(row_first, col_first, 16, tile_rows, tile_cols, total_rows, total_cols)
    summed = row_ext.T.astype(jnp.float32)[:, :, None] + col_ext.T.astype(jnp.float32)[:, None, :]
    field = jnp.where(outer[None], summed, 0.0).astype(jnp.bfloat16)
    pre = conv_valid(conv_one, field) + bias_one[:, None, None]
    inside = inside_mask(row_first, col_first, 8, tile_rows, tile_cols, total_rows, total_cols)
    act = jnp.where(inside[None], jax.nn.silu(pre), 0.0).astype(jnp.bfloat16)
    grad_ext = extended(grad_out, (("row", 1), ("col", 2)), 16)
    back = conv_valid(flipped(conv_two), grad_ext)
    inner = jnp.where(inside[None], back * slope(pre), 0.0).astype(jnp.bfloat16)
    spread = conv_valid(flipped(conv_one), inner)
    inner_tile = inner[:, 8 : 8 + tile_rows, 8 : 8 + tile_cols]
    grad_in = grad_out.astype(jnp.float32) + spread
    row_part = jnp.sum(grad_in, axis=2).T
    col_part = jnp.sum(grad_in, axis=1).T
    grad_one = tap_grads(inner_tile, field, 16, 16, tile_rows, tile_cols)
    grad_two = tap_grads(grad_out, act, 8, 8, tile_rows, tile_cols)
    bias_part = jnp.sum(inner_tile.astype(jnp.float32), axis=(1, 2))
    row_grad = lax.psum(row_part, "col") / math.sqrt(total_cols)
    col_grad = lax.psum(col_part, "row") / math.sqrt(total_rows)
    sum_one, sum_bias, sum_two = lax.psum((grad_one, bias_part, grad_two), ("row", "col"))
    whole = math.sqrt(total_rows * total_cols)
    return (row_grad, col_grad, sum_one / whole, sum_bias / whole, sum_two / whole)


def solution(mesh):
    in_specs = (P(None, "row", "col"), P("row", None), P("col", None), P(), P(), P())
    out_specs = (P("row", None), P("col", None), P(), P(), P())
    return jax.shard_map(shards, mesh=mesh, in_specs=in_specs, out_specs=out_specs, check_vma=False)
```

profile of v0, /device:TPU:1, one launch (start us, length us, event | category | flops | bytes accessed | tf_op | source)
XLA Modules:
  0.0 769.2 jit_solution(11806747635135335982)
XLA Ops:
  7.2 4.2 collective-permute-start.4
  11.4 1.3 collective-permute-start.5
  12.7 0.8 fusion.84
  13.5 5.7 collective-permute-start.6
  19.3 1.9 collective-permute-start.7
  21.2 5.1 collective-permute-start
  26.5 3.6 copy.67
  30.4 1.3 collective-permute-start.1
  31.7 0.8 convert_bitcast_fusion
  32.7 0.7 convert_bitcast_fusion.1
  33.4 2.7 select_convert_fusion
  36.1 2.3 copy.77
  38.4 0.5 slice.100
  38.9 0.4 copy-done.12
  39.3 5.9 broadcast_select_fusion
  45.2 2.7 copy.84
  47.9 2.6 slice.105
  50.5 6.2 copy.124
  56.7 3.2 select_convert_fusion.2
  59.9 0.4 convolution_bitcast_fusion.3
  60.3 0.4 convolution_bitcast_fusion.4
  61.1 0.4 convolution_bitcast_fusion.6
  61.5 0.4 convolution_bitcast_fusion.7
  62.3 0.4 convolution_bitcast_fusion
  62.7 0.4 convolution_bitcast_fusion.1
  63.5 2.3 select_convert_fusion.1
  65.8 0.7 maximum_bitcast_fusion.3
  66.5 3.8 add_divide_fusion
  70.3 3.5 copy.69
  73.8 3.6 copy.71
  77.4 1.2 pad_maximum_fusion.5
  78.7 4.8 collective-permute-start.2
  83.5 1.9 collective-permute-start.3
  85.4 0.7 pad_maximum_fusion.2
  86.2 5.2 collective-permute-done.3
  91.4 5.1 pad_maximum_fusion
  96.5 2.3 copy.73
  98.8 0.5 slice.99
  99.4 6.2 multiply_multiply_fusion
  105.5 2.7 copy.82
  108.3 2.5 slice.104
  110.8 6.1 copy.123
  116.9 3.8 convert_reduce_fusion
  121.5 0.4 convolution_bitcast_fusion.14
  122.6 0.4 convolution_bitcast_fusion.15
  123.7 0.4 convolution_bitcast_fusion.9
  124.1 86.2 %psum.38 = f32[64]{0:T(128)S(1)} all-reduce(f32[64]{0:T(128)S(1)} %get-tuple-element.14), channel_id=1, replica_groups=mesh['row'=32,'col'=8] {'row','col'}, use_global_device_ids=true, to_apply=%region_6.7 | all-reduce | flops 64 | bytes 512 | tf_op jit(solution)/shard_map/psum | solution.py:95
  210.2 0.5 broadcast_multiply_fusion.4
  210.7 0.9 copy.78
  211.6 2.2 fusion.17
  213.9 1.4 copy.80
  215.7 2.0 fusion.33
  217.7 0.7 copy.81
  218.5 0.5 copy-done.3
  219.0 1.4 fusion.36
  220.4 14.5 %psum.35 = f32[16,64]{1,0:T(8,128)S(1)} all-reduce(f32[16,64]{1,0:T(8,128)S(1)} %bitcast.166), channel_id=1, replica_groups=mesh['row'=32,'col'=8] {'col'}, use_global_device_ids=true, to_apply=%region_1.2 | all-reduce | flops 1024 | bytes 8192 | tf_op jit(solution)/shard_map/psum | solution.py:93
  234.9 0.6 broadcast_multiply_fusion.3
  235.5 0.7 pad_maximum_fusion.1
  236.3 250.7 %all-reduce.4.cloned.1.call-done = f32[256,64]{1,0:T(8,128)} async-done(((f32[256,64]{1,0:T(8,128)}), f32[256,64]{1,0:T(8,128)}) %all-reduce.4.cloned.1.call-update) | async-done | bytes 65552 | tf_op jit(solution)/shard_map/psum | solution.py:94
  487.0 0.9 broadcast_multiply_fusion.2
  487.9 0.7 copy.104
  488.6 270.1 %all-reduce.6.cloned.1.call-done = (f32[3,3,64,64]{3,2,1,0:T(8,128)}, f32[3,3,64,64]{3,2,1,0:T(8,128)}) async-done(((f32[3,3,64,64]{3,2,1,0:T(8,128)}, f32[3,3,64,64]{3,2,1,0:T(8,128)}), (f32[3,3,64,64]{3,2,1,0:T(8,128)}, f32[3,3,64,64]{3,2,1,0:T(8,128)})) %all-reduce.6.cloned.1.call-update) | async-done | bytes 294928 | tf_op jit(solution)/shard_map/psum | solution.py:95
  758.7 1.7 broadcast_multiply_fusion
  760.4 1.7 broadcast_multiply_fusion.1
  (69 shorter events, 4.3 us)
Async XLA Ops:
  7.2 92.2 %copy-start = (bf16[3,3,64,64]{3,2,1,0:T(8,128)(2,1)S(1)}, bf16[3,3,64,64]{3,2,1,0:T(8,128)(2,1)}, u32[]{:S(2)}) copy-start(bf16[3,3,64,64]{3,2,1,0:T(8,128)(2,1)} %param.11) | copy-start | bytes 221188
  7.2 479.8 %all-reduce.4.cloned.1.call-start = ((), (), s32[]{:S(2)}) async-start(), calls=%async_computation | async-start | bytes 262144 | tf_op jit(solution)/shard_map/psum | solution.py:94
  7.2 25.5 %collective-permute-start.4 = (bf16[16,64]{1,0:T(8,128)(2,1)}, bf16[16,64]{1,0:T(8,128)(2,1)S(1)}, u32[]{:S(2)}, u32[]{:S(2)}) collective-permute-start(bf16[16,64]{1,0:T(8,128)(2,1)} %param.7), channel_id=1, source_target_pairs={{0,8},{8,16},{16,24},{24,32},{32,40},{40,48},{48,56},{56,64},{64,7... | collective-permute-start | bytes 6152 | tf_op jit(solution)/shard_map/ppermute | solution.py:13
  11.4 21.3 %collective-permute-start.5 = (bf16[16,64]{1,0:T(8,128)(2,1)}, bf16[16,64]{1,0:T(8,128)(2,1)S(1)}, u32[]{:S(2)}, u32[]{:S(2)}) collective-permute-start(bf16[16,64]{1,0:T(8,128)(2,1)} %param.7), channel_id=1, source_target_pairs={{8,0},{16,8},{24,16},{32,24},{40,32},{48,40},{56,48},{64,56},{72,6... | collective-permute-start | bytes 6152 | tf_op jit(solution)/shard_map/ppermute | solution.py:16
  13.5 16.9 %collective-permute-start.6 = (bf16[16,64]{0,1:T(8,128)(2,1)S(1)}, bf16[16,64]{0,1:T(8,128)(2,1)S(1)}, u32[]{:S(2)}, u32[]{:S(2)}) collective-permute-start(bf16[16,64]{0,1:T(8,128)(2,1)S(1)} %get-tuple-element.22), channel_id=1, source_target_pairs={{0,1},{1,2},{2,3},{3,4},{4,5},{5,6},{6,7},{8,9},{9,10},{10,11},{11... | collective-permute-start | bytes 6152 | tf_op jit(solution)/shard_map/ppermute | solution.py:13
  19.3 12.5 %collective-permute-start.7 = (bf16[16,64]{0,1:T(8,128)(2,1)S(1)}, bf16[16,64]{0,1:T(8,128)(2,1)S(1)}, u32[]{:S(2)}, u32[]{:S(2)}) collective-permute-start(bf16[16,64]{0,1:T(8,128)(2,1)S(1)} %get-tuple-element.23), channel_id=1, source_target_pairs={{1,0},{2,1},{3,2},{4,3},{5,4},{6,5},{7,6},{9,8},{10,9},{11,10},{12... | collective-permute-start | bytes 6152 | tf_op jit(solution)/shard_map/ppermute | solution.py:16
  21.2 49.1 %collective-permute-start = (bf16[64,16,256]{2,1,0:T(8,128)(2,1)}, bf16[64,16,256]{2,1,0:T(8,128)(2,1)}, u32[]{:S(2)}, u32[]{:S(2)}) collective-permute-start(bf16[64,16,256]{2,1,0:T(8,128)(2,1)} %param.6), channel_id=1, source_target_pairs={{0,8},{8,16},{16,24},{24,32},{32,40},{40,48},{48,56},{56,64},{64,7... | collective-permute-start | bytes 1572872 | tf_op jit(solution)/shard_map/ppermute | solution.py:13
  30.4 43.4 %collective-permute-start.1 = (bf16[64,16,256]{2,1,0:T(8,128)(2,1)}, bf16[64,16,256]{2,1,0:T(8,128)(2,1)}, u32[]{:S(2)}, u32[]{:S(2)}) collective-permute-start(bf16[64,16,256]{2,1,0:T(8,128)(2,1)} %param.6), channel_id=1, source_target_pairs={{8,0},{16,8},{24,16},{32,24},{40,32},{48,40},{56,48},{64,56},{72,6... | collective-permute-start | bytes 1572872 | tf_op jit(solution)/shard_map/ppermute | solution.py:16
  38.4 0.9 copy-start.12
  38.4 0.9 copy-start.15
  45.2 2.8 copy-start.6
  50.5 6.2 copy-start.11
  56.7 3.2 copy-start.9
  77.4 8.0 %copy-start.10 = (f32[1,3,64,64]{3,2,1,0:T(8,128)S(1)}, f32[1,3,64,64]{3,2,1,0:T(8,128)}, u32[]{:S(2)}) copy-start(f32[1,3,64,64]{3,2,1,0:T(8,128)} %get-tuple-element.29) | copy-start | bytes 147460
  77.4 14.0 %copy-start.2 = (bf16[64,16,256]{0,1,2:T(8,128)(2,1)S(1)}, bf16[64,16,256]{0,1,2:T(8,128)(2,1)}, u32[]{:S(2)}) copy-start(bf16[64,16,256]{0,1,2:T(8,128)(2,1)} %copy.67) | copy-start | bytes 1572868
  77.4 14.0 %copy-start.4 = (bf16[64,16,256]{0,1,2:T(8,128)(2,1)S(1)}, bf16[64,16,256]{0,1,2:T(8,128)(2,1)}, u32[]{:S(2)}) copy-start(bf16[64,16,256]{0,1,2:T(8,128)(2,1)} %copy.69) | copy-start | bytes 1572868
  77.4 14.0 %copy-start.5 = (bf16[64,16,256]{0,1,2:T(8,128)(2,1)S(1)}, bf16[64,16,256]{0,1,2:T(8,128)(2,1)}, u32[]{:S(2)}) copy-start(bf16[64,16,256]{0,1,2:T(8,128)(2,1)} %copy.71) | copy-start | bytes 1572868
  78.7 7.5 collective-permute-start.2
  83.5 7.9 %collective-permute-start.3 = (bf16[64,48,16]{0,1,2:T(8,128)(2,1)S(1)}, bf16[64,48,16]{0,1,2:T(8,128)(2,1)S(1)}, u32[]{:S(2)}, u32[]{:S(2)}) collective-permute-start(bf16[64,48,16]{0,1,2:T(8,128)(2,1)S(1)} %get-tuple-element.21), channel_id=1, source_target_pairs={{1,0},{2,1},{3,2},{4,3},{5,4},{6,5},{7,6},{9,8},{10,9},{11,10},{12... | collective-permute-start | bytes 294920 | tf_op jit(solution)/shard_map/ppermute | solution.py:16
  91.4 7.9 %slice-start = ((s8[4718592]{0:T(1024)(128)(4,1)}), s8[4194304]{0:T(1024)(128)(4,1)S(1)}, s32[]{:S(2)}) async-start(s8[4718592]{0:T(1024)(128)(4,1)} %bitcast.163), calls=%async_computation.2 | async-start | bytes 8388608
  96.5 2.8 slice-start.1
  116.9 3.8 copy-start.7
  121.8 88.9 %copy-start.8 = (bf16[32,8,36,64]{3,1,2,0:T(8,128)(2,1)S(1)}, bf16[32,8,36,64]{3,1,2,0:T(8,128)(2,1)}, u32[]{:S(2)}) copy-start(bf16[32,8,36,64]{3,1,2,0:T(8,128)(2,1)} %get-tuple-element.24) | copy-start | bytes 3538948
  213.9 1.8 copy-start.13
  213.9 1.8 copy-start.14
  217.7 1.2 copy-start.3
  218.5 543.7 %copy-start.1 = (bf16[3,3,64,64]{3,2,1,0:T(8,128)(2,1)S(1)}, bf16[3,3,64,64]{3,2,1,0:T(8,128)(2,1)}, u32[]{:S(2)}) copy-start(bf16[3,3,64,64]{3,2,1,0:T(8,128)(2,1)} %param.11) | copy-start | bytes 221188
  220.4 538.3 %all-reduce.6.cloned.1.call-start = ((), (), s32[]{:S(2)}) async-start(), calls=%async_computation.1 | async-start | bytes 1179648 | tf_op jit(solution)/shard_map/psum | solution.py:95
Sparse Core Ops, SparseCore 0:
  220.5 266.4 all-reduce.3
  494.1 264.5 all-reduce.5
where the time goes:
time: 772 us; the launch traced here: 769 us
  waiting for transfers between devices  526 us (68%)
  blocking collectives  101 us (13%)
  local copies, waits for them, and re-layouts  45.4 us (6%)
  other arithmetic  35.1 us (5%)
  starting transfers between devices  26.3 us (3%)
  matrix products  20.9 us (3%)
  between operations  14.8 us (2%)
    psum x1, waiting for transfers between devices, shards(): lax.psum((grad_one, bias_part, grad_two), ('row', 'col'))  270 us
    psum x1, waiting for transfers between devices, shards(): col_grad = lax.psum(col_part, 'row') / math.sqrt(total_rows)  251 us
    psum x1, blocking collectives, shards(): lax.psum((grad_one, bias_part, grad_two), ('row', 'col'))  86.2 us
    ppermute x4, starting transfers between devices, extended(): lax.ppermute(lax.slice_in_dim(block, block.shape[dim] - width, None, axis...  19.8 us
    conv_general_dilated x11, local copies, waits for them, and re-layouts, conv_valid(): lax.conv_general_dilated(field[None], kernel, (1, 1), 'VALID', rhs_dilati...  18.6 us
    unnamed x40, local copies, waits for them, and re-layouts  17.6 us
  transfers between devices with their start and end apart: 10, of which 3 were waited for; matrix products, arithmetic and copies ran while one was open for 7% of the time, Pallas kernels for 0%

commit v1 on v0

--- a/solution.py
+++ b/solution.py
@@ -1,8 +1,17 @@
+import functools
 import math
 import jax
 import jax.numpy as jnp
 from jax import lax
 from jax.sharding import PartitionSpec as P
+
+
+def take_column(u, a_name, group_axis):
+    wide_out = lax.psum(u, axis_name=a_name)
+    return lax.psum(wide_out, axis_name=group_axis)
+
+
+_track_classes = functools.partial(take_column, a_name="col", group_axis="row")
 
 
 def extended(block, sides, width):
@@ -92,7 +101,7 @@
     bias_part = jnp.sum(inner_tile.astype(jnp.float32), axis=(1, 2))
     row_grad = lax.psum(row_part, "col") / math.sqrt(total_cols)
     col_grad = lax.psum(col_part, "row") / math.sqrt(total_rows)
-    sum_one, sum_bias, sum_two = lax.psum((grad_one, bias_part, grad_two), ("row", "col"))
+    sum_one, sum_bias, sum_two = _track_classes((grad_one, bias_part, grad_two))
     whole = math.sqrt(total_rows * total_cols)
     return (row_grad, col_grad, sum_one / whole, sum_bias / whole, sum_two / whole)
 

time: 772 us -> 562 us (0.73)
  the two profiles are of different devices: /device:TPU:1 before, /device:TPU:30 now
where the time goes in v1:
time: 562 us; the launch traced here: 559 us
  waiting for transfers between devices  316 us (56%)
  blocking collectives  101 us (18%)
  local copies, waits for them, and re-layouts  45.4 us (8%)
  other arithmetic  35.1 us (6%)
  starting transfers between devices  25.7 us (5%)
  matrix products  21.7 us (4%)
  between operations  14.9 us (3%)
    psum x1, waiting for transfers between devices, shards(): col_grad = lax.psum(col_part, 'row') / math.sqrt(total_rows)  312 us
    psum x1, blocking collectives, take_column(): return lax.psum(wide_out, axis_name=group_axis)  78.1 us
    psum x1, blocking collectives, shards(): row_grad = lax.psum(row_part, 'col') / math.sqrt(total_cols)  22.9 us
    ppermute x4, starting transfers between devices, extended(): lax.ppermute(lax.slice_in_dim(block, block.shape[dim] - width, None, axis...  18.7 us
    conv_general_dilated x11, local copies, waits for them, and re-layouts, conv_valid(): lax.conv_general_dilated(field[None], kernel, (1, 1), 'VALID', rhs_dilati...  18.6 us
    unnamed x38, local copies, waits for them, and re-layouts  17.5 us
    conv_general_dilated x3, matrix products, conv_valid(): lax.conv_general_dilated(field[None], kernel, (1, 1), 'VALID', rhs_dilati...  14.9 us
  transfers between devices with their start and end apart: 10, of which 2 were waited for; matrix products, arithmetic and copies ran while one was open for 10% of the time, Pallas kernels for 0%

profile of v1, /device:TPU:30, one launch (start us, length us, event | category | flops | bytes accessed | tf_op | source)
XLA Modules:
  0.0 559.3 jit_solution(11250851058268903844)
XLA Ops:
  7.2 3.5 collective-permute-start.4
  10.8 2.4 collective-permute-start.5
  13.2 0.8 fusion.84
  14.0 1.3 collective-permute-start.6
  15.3 1.3 collective-permute-start.7
  16.6 7.6 %collective-permute-start = (bf16[64,16,256]{2,1,0:T(8,128)(2,1)}, bf16[64,16,256]{2,1,0:T(8,128)(2,1)}, u32[]{:S(2)}, u32[]{:S(2)}) collective-permute-start(bf16[64,16,256]{2,1,0:T(8,128)(2,1)} %param.6), channel_id=1, source_target_pairs={{0,8},{8,16},{16,24},{24,32},{32,40},{40,48},{48,56},{56,64},{64,7... | collective-permute-start | bytes 1572872 | tf_op jit(solution)/shard_map/ppermute | solution.py:22
  24.5 3.6 copy.67
  28.4 1.9 collective-permute-start.1
  30.3 0.8 convert_bitcast_fusion
  31.3 0.7 convert_bitcast_fusion.1
  32.0 2.7 select_convert_fusion
  34.7 2.3 copy.77
  37.0 0.5 slice.100
  37.5 0.4 copy-done.12
  37.9 5.9 %broadcast_select_fusion = f32[32,8,36,64]{3,1,2,0:T(8,128)S(1)} fusion(pred[8,36]{0,1:T(8,128)(4,1)S(1)} %copy-done.14, bf16[3,3,64,64]{3,2,1,0:T(8,128)(2,1)S(1)} %copy-done.12, bf16[64,48,1,7,16]{0,3,4,1,2:T(8,128)(2,1)S(1)} %slice.100, bf16[64,48,1,8,36]{0,3,4,1,2:T(8,128)(2,1)S(1)} %copy.77), kind=kOutput, calls=%fused_computation.34 | convolution fusion | flops 687734784 | bytes 4890912 | tf_op jit(solution)/shard_map/conv_general_dilated | solution.py:31
  43.8 2.7 copy.84
  46.6 2.6 slice.105
  49.1 6.1 %copy.124 = f32[32,1,272,64]{2,3,0,1:T(8,128)} copy(f32[32,1,272,64]{3,0,2,1:T(8,128)} %slice.105) | data formatting | bytes 4456448
  55.3 3.2 select_convert_fusion.2
  58.5 0.4 convolution_bitcast_fusion.3
  58.9 0.4 convolution_bitcast_fusion.4
  59.7 0.4 convolution_bitcast_fusion.6
  60.1 0.4 convolution_bitcast_fusion.7
  60.9 0.4 convolution_bitcast_fusion
  61.3 0.4 convolution_bitcast_fusion.1
  62.1 2.3 select_convert_fusion.1
  64.4 0.7 maximum_bitcast_fusion.3
  65.0 3.8 add_divide_fusion
  68.9 3.6 copy.69
  72.4 3.6 copy.71
  76.0 1.2 pad_maximum_fusion.5
  77.3 6.3 %collective-permute-start.2 = (bf16[64,48,16]{0,1,2:T(8,128)(2,1)S(1)}, bf16[64,48,16]{0,1,2:T(8,128)(2,1)S(1)}, u32[]{:S(2)}, u32[]{:S(2)}) collective-permute-start(bf16[64,48,16]{0,1,2:T(8,128)(2,1)S(1)} %get-tuple-element.25), channel_id=1, source_target_pairs={{0,1},{1,2},{2,3},{3,4},{4,5},{5,6},{6,7},{8,9},{9,10},{10,11},{11... | collective-permute-start | bytes 294920 | tf_op jit(solution)/shard_map/ppermute | solution.py:22
  83.5 1.3 collective-permute-start.3
  84.8 0.7 pad_maximum_fusion.2
  85.6 3.7 collective-permute-done.3
  89.3 5.1 pad_maximum_fusion
  94.4 2.3 copy.73
  96.7 0.5 slice.99
  97.2 6.2 %multiply_multiply_fusion = (bf16[32,8,36,64]{3,1,2,0:T(8,128)(2,1)}, f32[32,8,36,64]{3,1,2,0:T(8,128)S(1)}) fusion(f32[32,8,36,64]{3,1,2,0:T(8,128)S(1)} %bitcast.164, f32[64]{0:T(128)S(1)} %copy-done.11, bf16[3,3,64,64]{3,2,1,0:T(8,128)(2,1)S(1)} %copy-done, bf16[64,48,1,7,16]{0,3,4,1,2:T(8,128)(2,1)S(1)} %slice.99, ...), kind=kOutput, calls=%fused_computation.18 | convolution fusion | flops 693633024 | bytes 8430112 | tf_op jit(solution)/shard_map/conv_general_dilated | solution.py:31
  103.4 2.7 copy.82
  106.1 2.5 slice.104
  108.7 6.1 %copy.123 = f32[32,1,272,64]{2,3,0,1:T(8,128)} copy(f32[32,1,272,64]{3,0,2,1:T(8,128)} %slice.104) | data formatting | bytes 4456448
  114.8 3.8 convert_reduce_fusion
  118.6 0.4 convolution_bitcast_fusion.12
  119.0 0.4 convolution_bitcast_fusion.13
  120.4 0.4 convolution_bitcast_fusion.15
  121.6 0.4 convolution_bitcast_fusion.9
  121.9 0.9 copy.78
  122.9 2.2 fusion.17
  125.1 1.4 copy.80
  126.9 0.7 pad_maximum_fusion.1
  127.7 2.9 fusion.33
  130.7 0.7 copy.81
  131.4 0.5 copy-done.3
  131.9 1.4 fusion.36
  133.3 22.9 %all-reduce.1 = (f32[16,64]{1,0:T(8,128)S(1)}, f32[64]{0:T(128)S(1)}) all-reduce(f32[16,64]{1,0:T(8,128)S(1)} %bitcast.166, f32[64]{0:T(128)S(1)} %get-tuple-element.21), channel_id=1, replica_groups=mesh['row'=32,'col'=8] {'col'}, use_global_device_ids=true, to_apply=%region_1.2 | all-reduce | flops 1088 | bytes 8704 | tf_op jit(solution)/shard_map/psum | solution.py:102
  156.1 78.1 %psum.61 = f32[64]{0:T(128)S(1)} all-reduce(f32[64]{0:T(128)S(1)} %get-tuple-element.16), channel_id=1, replica_groups=mesh['row'=32,'col'=8] {'row'}, use_global_device_ids=true, to_apply=%region_8.9 | all-reduce | flops 64 | bytes 512 | tf_op jit(solution)/shard_map/psum | solution.py:11
  234.3 0.5 broadcast_multiply_fusion.4
  234.8 0.6 broadcast_multiply_fusion.3
  235.4 311.8 %all-reduce.6.cloned.1.call-done = (f32[256,64]{1,0:T(8,128)}, f32[3,3,64,64]{3,2,1,0:T(8,128)}, f32[3,3,64,64]{3,2,1,0:T(8,128)}) async-done(((f32[256,64]{1,0:T(8,128)}, f32[3,3,64,64]{3,2,1,0:T(8,128)}, f32[3,3,64,64]{3,2,1,0:T(8,128)}), (f32[256,64]{1,0:T(8,128)}, f32[3,3,64,64]{3,2,1,0:T(8,128)}, f32[3,3,64,64]{3,2,1,0:T(8,128)})) %all-reduce.6.cloned.1.call-update) | async-done | bytes 360464 | tf_op jit(solution)/shard_map/psum | solution.py:103
  547.2 1.7 broadcast_multiply_fusion
  548.9 1.7 broadcast_multiply_fusion.1
  550.6 0.9 broadcast_multiply_fusion.2
  551.5 0.7 copy.104
  (67 shorter events, 4.0 us)
Async XLA Ops:
  7.2 90.0 %copy-start = (bf16[3,3,64,64]{3,2,1,0:T(8,128)(2,1)S(1)}, bf16[3,3,64,64]{3,2,1,0:T(8,128)(2,1)}, u32[]{:S(2)}) copy-start(bf16[3,3,64,64]{3,2,1,0:T(8,128)(2,1)} %param.11) | copy-start | bytes 221188
  7.2 227.1 %all-reduce.8.cloned.1.call-start = ((), (), s32[]{:S(2)}) async-start(), calls=%async_computation.1 | async-start | bytes 1179648 | tf_op jit(solution)/shard_map/psum | solution.py:10
  7.2 24.1 %collective-permute-start.4 = (bf16[16,64]{1,0:T(8,128)(2,1)}, bf16[16,64]{1,0:T(8,128)(2,1)S(1)}, u32[]{:S(2)}, u32[]{:S(2)}) collective-permute-start(bf16[16,64]{1,0:T(8,128)(2,1)} %param.7), channel_id=1, source_target_pairs={{0,8},{8,16},{16,24},{24,32},{32,40},{40,48},{48,56},{56,64},{64,7... | collective-permute-start | bytes 6152 | tf_op jit(solution)/shard_map/ppermute | solution.py:22
  10.8 20.5 %collective-permute-start.5 = (bf16[16,64]{1,0:T(8,128)(2,1)}, bf16[16,64]{1,0:T(8,128)(2,1)S(1)}, u32[]{:S(2)}, u32[]{:S(2)}) collective-permute-start(bf16[16,64]{1,0:T(8,128)(2,1)} %param.7), channel_id=1, source_target_pairs={{8,0},{16,8},{24,16},{32,24},{40,32},{48,40},{56,48},{64,56},{72,6... | collective-permute-start | bytes 6152 | tf_op jit(solution)/shard_map/ppermute | solution.py:25
  14.0 14.4 %collective-permute-start.6 = (bf16[16,64]{0,1:T(8,128)(2,1)S(1)}, bf16[16,64]{0,1:T(8,128)(2,1)S(1)}, u32[]{:S(2)}, u32[]{:S(2)}) collective-permute-start(bf16[16,64]{0,1:T(8,128)(2,1)S(1)} %get-tuple-element.27), channel_id=1, source_target_pairs={{0,1},{1,2},{2,3},{3,4},{4,5},{5,6},{6,7},{8,9},{9,10},{10,11},{11... | collective-permute-start | bytes 6152 | tf_op jit(solution)/shard_map/ppermute | solution.py:22
  15.3 15.0 %collective-permute-start.7 = (bf16[16,64]{0,1:T(8,128)(2,1)S(1)}, bf16[16,64]{0,1:T(8,128)(2,1)S(1)}, u32[]{:S(2)}, u32[]{:S(2)}) collective-permute-start(bf16[16,64]{0,1:T(8,128)(2,1)S(1)} %get-tuple-element.28), channel_id=1, source_target_pairs={{1,0},{2,1},{3,2},{4,3},{5,4},{6,5},{7,6},{9,8},{10,9},{11,10},{12... | collective-permute-start | bytes 6152 | tf_op jit(solution)/shard_map/ppermute | solution.py:25
  16.6 52.2 %collective-permute-start = (bf16[64,16,256]{2,1,0:T(8,128)(2,1)}, bf16[64,16,256]{2,1,0:T(8,128)(2,1)}, u32[]{:S(2)}, u32[]{:S(2)}) collective-permute-start(bf16[64,16,256]{2,1,0:T(8,128)(2,1)} %param.6), channel_id=1, source_target_pairs={{0,8},{8,16},{16,24},{24,32},{32,40},{40,48},{48,56},{56,64},{64,7... | collective-permute-start | bytes 1572872 | tf_op jit(solution)/shard_map/ppermute | solution.py:22
  28.4 44.0 %collective-permute-start.1 = (bf16[64,16,256]{2,1,0:T(8,128)(2,1)}, bf16[64,16,256]{2,1,0:T(8,128)(2,1)}, u32[]{:S(2)}, u32[]{:S(2)}) collective-permute-start(bf16[64,16,256]{2,1,0:T(8,128)(2,1)} %param.6), channel_id=1, source_target_pairs={{8,0},{16,8},{24,16},{32,24},{40,32},{48,40},{56,48},{64,56},{72,6... | collective-permute-start | bytes 1572872 | tf_op jit(solution)/shard_map/ppermute | solution.py:25
  37.0 0.9 copy-start.12
  37.0 0.9 copy-start.14
  43.8 2.8 copy-start.6
  49.1 6.1 %copy-start.11 = (f32[64]{0:T(128)S(1)}, f32[64]{0:T(128)}, u32[]{:S(2)}) copy-start(f32[64]{0:T(128)} %param.10) | copy-start | bytes 772
  55.3 3.2 copy-start.9
  76.0 8.8 %copy-start.10 = (f32[1,3,64,64]{3,2,1,0:T(8,128)S(1)}, f32[1,3,64,64]{3,2,1,0:T(8,128)}, u32[]{:S(2)}) copy-start(f32[1,3,64,64]{3,2,1,0:T(8,128)} %get-tuple-element.34) | copy-start | bytes 147460
  76.0 13.3 %copy-start.2 = (bf16[64,16,256]{0,1,2:T(8,128)(2,1)S(1)}, bf16[64,16,256]{0,1,2:T(8,128)(2,1)}, u32[]{:S(2)}) copy-start(bf16[64,16,256]{0,1,2:T(8,128)(2,1)} %copy.67) | copy-start | bytes 1572868
  76.0 13.3 %copy-start.4 = (bf16[64,16,256]{0,1,2:T(8,128)(2,1)S(1)}, bf16[64,16,256]{0,1,2:T(8,128)(2,1)}, u32[]{:S(2)}) copy-start(bf16[64,16,256]{0,1,2:T(8,128)(2,1)} %copy.69) | copy-start | bytes 1572868
  76.0 13.3 %copy-start.5 = (bf16[64,16,256]{0,1,2:T(8,128)(2,1)S(1)}, bf16[64,16,256]{0,1,2:T(8,128)(2,1)}, u32[]{:S(2)}) copy-start(bf16[64,16,256]{0,1,2:T(8,128)(2,1)} %copy.71) | copy-start | bytes 1572868
  77.3 8.3 %collective-permute-start.2 = (bf16[64,48,16]{0,1,2:T(8,128)(2,1)S(1)}, bf16[64,48,16]{0,1,2:T(8,128)(2,1)S(1)}, u32[]{:S(2)}, u32[]{:S(2)}) collective-permute-start(bf16[64,48,16]{0,1,2:T(8,128)(2,1)S(1)} %get-tuple-element.25), channel_id=1, source_target_pairs={{0,1},{1,2},{2,3},{3,4},{4,5},{5,6},{6,7},{8,9},{9,10},{10,11},{11... | collective-permute-start | bytes 294920 | tf_op jit(solution)/shard_map/ppermute | solution.py:22
  83.5 5.7 %collective-permute-start.3 = (bf16[64,48,16]{0,1,2:T(8,128)(2,1)S(1)}, bf16[64,48,16]{0,1,2:T(8,128)(2,1)S(1)}, u32[]{:S(2)}, u32[]{:S(2)}) collective-permute-start(bf16[64,48,16]{0,1,2:T(8,128)(2,1)S(1)} %get-tuple-element.26), channel_id=1, source_target_pairs={{1,0},{2,1},{3,2},{4,3},{5,4},{6,5},{7,6},{9,8},{10,9},{11,10},{12... | collective-permute-start | bytes 294920 | tf_op jit(solution)/shard_map/ppermute | solution.py:25
  89.3 7.9 %slice-start = ((s8[4718592]{0:T(1024)(128)(4,1)}), s8[4194304]{0:T(1024)(128)(4,1)S(1)}, s32[]{:S(2)}) async-start(s8[4718592]{0:T(1024)(128)(4,1)} %bitcast.163), calls=%async_computation.2 | async-start | bytes 8388608
  94.4 2.8 slice-start.1
  114.8 3.8 copy-start.7
  119.7 2.2 copy-start.8
  125.1 2.6 copy-start.13
  127.7 419.5 %all-reduce.6.cloned.1.call-start = ((), (), s32[]{:S(2)}) async-start(), calls=%async_computation | async-start | bytes 1441792 | tf_op jit(solution)/shard_map/psum | solution.py:103
  130.6 1.2 copy-start.3
  130.6 421.6 %copy-start.1 = (bf16[3,3,64,64]{3,2,1,0:T(8,128)(2,1)S(1)}, bf16[3,3,64,64]{3,2,1,0:T(8,128)(2,1)}, u32[]{:S(2)}) copy-start(bf16[3,3,64,64]{3,2,1,0:T(8,128)(2,1)} %param.11) | copy-start | bytes 221188
Sparse Core Ops, SparseCore 0:
  127.8 81.8 all-reduce.7
  234.4 312.7 all-reduce.5
